TPU v7x, 512 devices: a whole 4x8x8 slice. The times are simulated.
512 devices in a mesh: rx: 32 (over z, y_lo, core), freq: 16 (over y_hi, x).
Axes of the slice: x: 4, y: 8 (y_hi: 4, y_lo: 2; y = y_hi * 2 + y_lo), z: 8, core: 2. Of those that a mesh axis runs over, the one named last changes fastest.
Arguments:
- spectra: bfloat16 [2, 128, 32, 8192], P(None, 'freq', None, 'rx'), may hold values from -60 to 60
- source_block: int32 [1], replicated, may hold values from 0 to 31
Outputs:
- correlations: bfloat16 [256, 256, 8192], P(None, 'freq', 'rx')
All inputs are finite; a program needn't handle non-finite values.
Results may differ from a plain program's by a relative error of at most 0.0057.
Values may be sent and summed in bfloat16 or wider, within the bound.
A program may use at most 64 MiB of HBM per device.

v0:
```python
import math

import jax
import jax.numpy as jnp
from jax import lax
from jax.sharding import PartitionSpec as P

F = 128
W = 32
LAGS = 256


def extended(cells, sides, width):
    for axis, dim in sides:
        count = lax.axis_size(axis)
        ends = count - 1
        head = lax.slice_in_dim(cells, 0, width, axis=dim)
        tail = lax.slice_in_dim(cells, cells.shape[dim] - width, cells.shape[dim], axis=dim)
        cells = jnp.concatenate(
            [
                lax.ppermute(tail, axis, [(i, (i + 1) % count) for i in range(ends)]),
                cells,
                lax.ppermute(head, axis, [((i + 1) % count, i) for i in range(ends)]),
            ],
            axis=dim,
        )
    return cells


def broadcast(value, axis, source):
    kept = jnp.where(lax.axis_index(axis) == source, value, 0).astype(value.dtype)
    return lax.psum(kept, axis)


def whiten(planes_in):
    planes = planes_in.astype(jnp.float32)
    magnitude = jnp.sqrt(planes[0] * planes[0] + planes[1] * planes[1])
    padded = extended(magnitude, (("freq", 0),), 1)
    smooth = (padded[:-2] + padded[1:-1] + padded[2:]) / 3.0
    divisor = jnp.maximum(smooth, 0.5)
    return (planes / divisor[None]).astype(jnp.bfloat16)


def build_lag_basis():
    bins = jnp.arange(F, dtype=jnp.int32)
    lagged = jnp.arange(LAGS, dtype=jnp.int32)
    phase = bins[:, None] * lagged[None, :] % LAGS
    angle = phase.astype(jnp.float32) * (2.0 * math.pi / LAGS)
    return jnp.concatenate([jnp.cos(angle), -jnp.sin(angle)], axis=0).astype(jnp.bfloat16)


def window_products(sent, white):
    joined_sources = jnp.concatenate([sent[0], sent[1]], axis=1)
    leading_operand = jnp.concatenate([white[0], white[1]], axis=1)
    trailing_operand = jnp.concatenate([white[1], -white[0]], axis=1)
    real_total = jnp.einsum(
        "pgo,pgd->pod", joined_sources, leading_operand, preferred_element_type=jnp.float32
    )
    imaginary_total = jnp.einsum(
        "pgo,pgd->pod", joined_sources, trailing_operand, preferred_element_type=jnp.float32
    )
    return (real_total, imaginary_total)


def transform(cross_part, basis_table):
    stacked = cross_part.reshape(2 * F, cross_part.shape[2], cross_part.shape[3])
    lagged = jnp.einsum("kl,ksr->slr", basis_table, stacked, preferred_element_type=jnp.float32) * (
        2.0 / F
    )
    return lagged.astype(jnp.bfloat16)


def on_device(spectra, source_block):
    white = whiten(spectra)
    owner = source_block[0]
    sent = broadcast(white, "rx", owner)
    real_total, imaginary_total = window_products(sent, white)
    cross = (jnp.stack([real_total, imaginary_total]) / W).astype(jnp.bfloat16)
    basis_table = build_lag_basis()
    spread = lax.all_to_all(cross, "freq", split_axis=2, concat_axis=1, tiled=True)
    lagged = transform(spread, basis_table)
    result = lax.all_to_all(lagged, "freq", split_axis=1, concat_axis=0, tiled=True)
    return result


def solution(mesh):
    in_specs = (P(None, "freq", None, "rx"), P())
    out_specs = P(None, "freq", "rx")
    return jax.shard_map(
        on_device, mesh=mesh, in_specs=in_specs, out_specs=out_specs, check_vma=False
    )
```

profile of v0, /device:TPU:1, one launch (start us, length us, event | category | flops | bytes accessed | tf_op | source)
XLA Modules:
  0.0 392.1 jit_solution(4345271281972983025)
XLA Ops:
  6.5 0.0 copy-start
  6.5 0.0 all-reduce.2.cloned.1.call-start
  6.5 1.1 convert_element_type.23
  7.6 0.1 fusion.10
  7.7 3.9 %collective-permute-start = (f32[1,32,256]{2,1,0:T(8,128)S(1)}, f32[1,32,256]{2,1,0:T(8,128)S(1)}, u32[]{:S(2)}, u32[]{:S(2)}) collective-permute-start(f32[1,32,256]{2,1,0:T(8,128)S(1)} %get-tuple-element.11), channel_id=1, source_target_pairs={{0,1},{1,2},{2,3},{3,4},{4,5},{5,6},{6,7},{7,8},{8,9},{9,10},{10,1... | collective-permute-start | bytes 98312 | tf_op jit(solution)/shard_map/ppermute | solution.py:21
  11.7 1.3 collective-permute-start.1
  13.0 0.1 fusion.29
  13.7 0.0 collective-permute-done
  13.7 2.6 collective-permute-done.1
  16.4 0.0 copy-done
  16.4 0.8 broadcast_select_fusion
  17.2 0.0 all-reduce.2.cloned.1.call-update
  17.3 237.6 %all-reduce.2.cloned.1.call-done = bf16[2,8,32,256]{3,2,1,0:T(8,128)(2,1)} async-done(((bf16[2,8,32,256]{3,2,1,0:T(8,128)(2,1)}), bf16[2,8,32,256]{3,2,1,0:T(8,128)(2,1)}) %all-reduce.2.cloned.1.call-update) | async-done | bytes 262160 | tf_op jit(solution)/shard_map/psum | solution.py:32
  254.9 1.0 slice_bitcast_fusion.3
  255.8 0.5 convolution_bitcast_fusion.1
  256.3 0.5 convolution_bitcast_fusion
  256.8 0.5 fusion
  257.3 2.5 copy.17
  259.8 8.1 %all-to-all-start = ((bf16[2,8,256,256]{3,1,0,2:T(8,128)(2,1)}), bf16[2,8,256,256]{3,1,0,2:T(8,128)(2,1)S(1)}, u32[]{:S(2)}, u32[]{:S(2)}) async-start(bf16[2,8,256,256]{3,1,0,2:T(8,128)(2,1)} %copy.17), calls=%async_computation | async-start | bytes 4194304 | tf_op jit(solution)/shard_map/all_to_all | solution.py:80
  267.9 0.5 negate_convert_fusion
  268.4 52.8 %all-to-all-done = bf16[2,8,256,256]{3,1,0,2:T(8,128)(2,1)S(1)} async-done(((bf16[2,8,256,256]{3,1,0,2:T(8,128)(2,1)}), bf16[2,8,256,256]{3,1,0,2:T(8,128)(2,1)S(1)}, u32[]{:S(2)}, u32[]{:S(2)}) %all-to-all-start) | async-done | bytes 2097184 | tf_op jit(solution)/shard_map/all_to_all | solution.py:80
  321.3 0.7 copy.19
  322.0 3.0 fusion.2
  325.0 3.3 copy.21
  328.3 54.7 %all_to_all.33 = bf16[16,256,256]{2,0,1:T(8,128)(2,1)S(1)} all-to-all(bf16[16,256,256]{2,0,1:T(8,128)(2,1)S(1)} %copy.21), channel_id=1, replica_groups=mesh['rx'=32,'freq'=16] {'freq'}, dimensions={1} | all-to-all | bytes 4194304 | tf_op jit(solution)/shard_map/all_to_all | solution.py:82
  383.1 2.2 copy.23
  (4 shorter events, 0.1 us)
Async XLA Ops:
  6.5 9.8 %copy-start = (bf16[2,8,32,256]{3,2,1,0:T(8,128)(2,1)S(1)}, bf16[2,8,32,256]{3,2,1,0:T(8,128)(2,1)}, u32[]{:S(2)}) copy-start(bf16[2,8,32,256]{3,2,1,0:T(8,128)(2,1)} %param.2) | copy-start | bytes 786436
  6.5 248.3 %all-reduce.2.cloned.1.call-start = ((), (), s32[]{:S(2)}) async-start(), calls=%async_computation.2 | async-start | bytes 524288 | tf_op jit(solution)/shard_map/psum | solution.py:32
  7.7 6.0 %collective-permute-start = (f32[1,32,256]{2,1,0:T(8,128)S(1)}, f32[1,32,256]{2,1,0:T(8,128)S(1)}, u32[]{:S(2)}, u32[]{:S(2)}) collective-permute-start(f32[1,32,256]{2,1,0:T(8,128)S(1)} %get-tuple-element.11), channel_id=1, source_target_pairs={{0,1},{1,2},{2,3},{3,4},{4,5},{5,6},{6,7},{7,8},{8,9},{9,10},{10,1... | collective-permute-start | bytes 98312 | tf_op jit(solution)/shard_map/ppermute | solution.py:21
  11.7 4.7 %collective-permute-start.1 = (f32[1,32,256]{2,1,0:T(8,128)S(1)}, f32[1,32,256]{2,1,0:T(8,128)S(1)}, u32[]{:S(2)}, u32[]{:S(2)}) collective-permute-start(f32[1,32,256]{2,1,0:T(8,128)S(1)} %get-tuple-element.12), channel_id=1, source_target_pairs={{1,0},{2,1},{3,2},{4,3},{5,4},{6,5},{7,6},{8,7},{9,8},{10,9},{11,1... | collective-permute-start | bytes 98312 | tf_op jit(solution)/shard_map/ppermute | solution.py:23
  259.8 61.5 %all-to-all-start = ((bf16[2,8,256,256]{3,1,0,2:T(8,128)(2,1)}), bf16[2,8,256,256]{3,1,0,2:T(8,128)(2,1)S(1)}, u32[]{:S(2)}, u32[]{:S(2)}) async-start(bf16[2,8,256,256]{3,1,0,2:T(8,128)(2,1)} %copy.17), calls=%async_computation | async-start | bytes 4194304 | tf_op jit(solution)/shard_map/all_to_all | solution.py:80
Sparse Core Ops, SparseCore 0:
  17.4 237.4 all-reduce.1
where the time goes:
time: 392 us
  waiting for transfers between devices  293 us (75%)
  blocking collectives  54.7 us (14%)
  between operations  14.2 us (4%)
  starting transfers between devices  13.3 us (3%)
  local copies, waits for them, and re-layouts  9.73 us (2%)
  matrix products  4 us (1%)
    psum x1, waiting for transfers between devices, broadcast(): return lax.psum(kept, axis)  238 us
    all_to_all x1, blocking collectives, on_device(): lax.all_to_all(lagged, 'freq', split_axis=1, concat_axis=0, tiled=True)  54.7 us
    all_to_all x1, waiting for transfers between devices, on_device(): lax.all_to_all(cross, 'freq', split_axis=2, concat_axis=1, tiled=True)  52.8 us
    all_to_all x1, starting transfers between devices, on_device(): lax.all_to_all(cross, 'freq', split_axis=2, concat_axis=1, tiled=True)  8.08 us
  transfers between devices with their start and end apart: 4, of which 3 were waited for; matrix products, arithmetic and copies ran while one was open for 0% of the time, Pallas kernels for 0%

commit v1 on v0

v1 whole, which is shorter than its diff:
```python
import functools
import math

import jax
import jax.numpy as jnp
import numpy as np
from jax import lax
from jax.experimental import pallas as pl
from jax.experimental.pallas import tpu as pltpu
from jax.sharding import PartitionSpec as P

F = 128
W = 32
LAGS = 256
NX, NYH, NYL, NZ, NC = 4, 4, 2, 8, 2
NK = NX * NYH
FB = F // NK
LB = LAGS // NK
MESH = pl.DeviceIdType.MESH


def mod(a, n):
    return lax.rem(a + n, n)


def kernel(owner_ref, tw_ref, spec_ref, out_ref, halo, st_own, b1, b1s, b2, sg, rg, rg1, cosb, sinb, lhs, acc,
           halo_send, halo_recv, s1_send, s1_recv, s2_send, s2_recv, sx_send, sx_recv, sy_send, sy_recv,
           z_send, z_recv, c_send, c_recv, ry_send, ry_recv, rx_send, rx_recv):
    r = lax.axis_index("rx")
    k = lax.axis_index("freq")
    z = lax.div(r, 4)
    q = lax.rem(r, 4)
    yl = lax.div(q, 2)
    core = lax.rem(q, 2)
    yh = lax.div(k, 4)
    x = lax.rem(k, 4)

    def dev(z_, yl_, c_, yh_, x_):
        return (z_ * 4 + yl_ * 2 + c_, yh_ * 4 + x_)

    def remote(src, dst, send, recv, device):
        copy = pltpu.make_async_remote_copy(src, dst, send, recv, device_id=device, device_id_type=MESH)
        copy.start()
        return copy

    halo_peers = [(r, mod(k + 1, NK)), (r, mod(k - 1, NK))]
    q_peers = [(z * 4 + lax.rem(q + d, 4), k) for d in range(1, 4)]
    z_peers = [(lax.rem(z + d, NZ) * 4 + q, k) for d in range(1, NZ)]
    x_peers = [dev(z, yl, core, yh, lax.rem(x + d, NX)) for d in range(1, NX)]
    y = yh * 2 + yl
    y_peers = []
    for d in range(1, 8):
        yy = lax.rem(y + d, 8)
        y_peers.append(dev(z, lax.rem(yy, 2), core, lax.div(yy, 2), x))
    everyone = halo_peers + q_peers + z_peers + x_peers + y_peers

    barrier = pltpu.get_barrier_semaphore()
    for peer in everyone:
        pl.semaphore_signal(barrier, inc=1, device_id=peer, device_id_type=MESH)
    pl.semaphore_wait(barrier, len(everyone))

    up, down = halo_peers
    h0 = remote(spec_ref.at[:, FB - 1], halo.at[0], halo_send.at[0], halo_recv.at[0], up)
    h1 = remote(spec_ref.at[:, 0], halo.at[1], halo_send.at[1], halo_recv.at[1], down)

    lane = lax.broadcasted_iota(jnp.int32, (8, FB * W), 1)
    lag = lax.broadcasted_iota(jnp.int32, (8, FB * W), 0) + k * LB

    @pl.loop(0, NK)
    def _(kk):
        bins = kk * FB + lax.shift_right_logical(lane, 5)
        angle = jnp.bitwise_and(bins * lag, LAGS - 1).astype(jnp.float32) * (2.0 * math.pi / LAGS)
        cosb[kk] = jnp.cos(angle)
        sinb[kk] = jnp.sin(angle)

    h0.wait()
    h1.wait()

    def magnitude(a, b):
        return jnp.sqrt(a * a + b * b)

    lower = halo[0].astype(jnp.float32)
    upper = halo[1].astype(jnp.float32)
    m_low = jnp.where(k == 0, 0.0, magnitude(lower[0], lower[1]))
    m_high = jnp.where(k == NK - 1, 0.0, magnitude(upper[0], upper[1]))

    def raw(p, f):
        return spec_ref[p, f].astype(jnp.float32)

    mags = [m_low] + [magnitude(raw(0, f), raw(1, f)) for f in range(FB)] + [m_high]
    for f in range(FB):
        divisor = jnp.maximum((mags[f] + mags[f + 1] + mags[f + 2]) / 3.0, 0.5)
        for p in range(2):
            rg[k, pl.ds(p * 256 + f * W, W), :] = (raw(p, f) / divisor).astype(jnp.bfloat16)

    sends = []

    def ry(slot, block, rows, device):
        view = rg.at[block, rows]
        return remote(view, view, ry_send.at[slot], ry_recv.at[slot], device)

    def rx(row, slot, block, rows, device):
        view = rg.at[block, rows]
        return remote(view, view, rx_send.at[row, slot], rx_recv.at[row, slot], device)

    every = pl.ds(0, 512)
    first, second = pl.ds(0, 256), pl.ds(256, 256)
    y_up = dev(z, yl, core, mod(yh + 1, NYH), x)
    y_dn = dev(z, yl, core, mod(yh - 1, NYH), x)
    x_up = dev(z, yl, core, yh, mod(x + 1, NX))
    x_dn = dev(z, yl, core, yh, mod(x - 1, NX))

    def block_of(dyh, dx):
        return mod(yh + dyh, NYH) * NX + mod(x + dx, NX)

    for p in range(2):
        t = rg[k, pl.ds(p * 256, 256), :].astype(jnp.float32).T.reshape(NZ, 4, 8, FB * W)
        for j in range(4):
            st_own[j, :, pl.ds(p * 8, 8), :] = t[:, j].astype(jnp.bfloat16)
    s1 = [remote(st_own.at[lax.rem(q + d, 4)], b1.at[q], s1_send.at[d], s1_recv.at[d], q_peers[d - 1])
          for d in range(1, 4)]
    y_own = [ry(0, k, every, y_up), ry(1, k, every, y_dn)]
    x_own = [rx(0, 0, k, every, x_up), rx(0, 1, k, every, x_dn)]
    b1[q] = st_own[q]
    for c in s1:
        c.wait()
    owner = owner_ref[0]
    b1s[...] = b1[lax.rem(owner, 4)]
    s2 = [remote(b1s.at[lax.rem(z + d, NZ)], b2.at[z], s2_send.at[d], s2_recv.at[d], z_peers[d - 1])
          for d in range(1, NZ)]
    b2[z] = b1s[z]
    for c in s2:
        c.wait()
    sg[z, core, yl, k] = b2[lax.div(owner, 4)]
    mine = sg.at[z, core, yl, k]
    sx = [remote(mine, mine, sx_send.at[d], sx_recv.at[d], x_peers[d - 1]) for d in range(1, NX)]
    for c in sx:
        c.wait()
    row = sg.at[z, core, yl, pl.ds(yh * NX, NX)]
    sy = [remote(row, row, sy_send.at[d], sy_recv.at[d], y_peers[d - 1]) for d in range(1, 8)]
    for c in sy:
        c.wait()

    z_up = dev(mod(z + 1, NZ), yl, core, yh, x)
    z_dn = dev(mod(z - 1, NZ), yl, core, yh, x)
    sibling = dev(z, yl, 1 - core, yh, x)

    def zstep(t):
        a = sg.at[mod(z - t, NZ), core]
        b = sg.at[mod(z + t, NZ), core]
        if t == 3:
            a, b = a.at[0], b.at[1]
        return [remote(a, a, z_send.at[0, t], z_recv.at[0, t], z_up),
                remote(b, b, z_send.at[1, t], z_recv.at[1, t], z_dn)]

    def share(slot, zz):
        view = sg.at[zz, core]
        return remote(view, view, c_send.at[slot], c_recv.at[slot], sibling)

    zs = zstep(0)
    cs = [share(0, z)]

    for c in y_own:
        c.wait_recv()
    sends += y_own
    y_far = [ry(2, block_of(-1, 0), first, y_up), ry(3, block_of(1, 0), second, y_dn)]
    x_next = [[rx(1, 0, block_of(-1, 0), every, x_up), rx(1, 1, block_of(-1, 0), every, x_dn)],
              [rx(2, 0, block_of(1, 0), every, x_up), rx(2, 1, block_of(1, 0), every, x_dn)]]
    for c in x_own:
        c.wait_recv()
    sends += x_own
    fars = [[rx(0, 2, block_of(0, -1), first, x_up), rx(0, 3, block_of(0, 1), second, x_dn)]]
    for c in zs:
        c.wait_recv()
    sends += zs
    zs = zstep(1)
    cs += [share(1, mod(z - 1, NZ)), share(2, mod(z + 1, NZ))]
    for c in y_far:
        c.wait_recv()
    sends += y_far
    x_next.append([rx(3, 0, block_of(2, 0), every, x_up), rx(3, 1, block_of(2, 0), every, x_dn)])
    for c in zs:
        c.wait_recv()
    sends += zs
    zs = zstep(2)
    cs += [share(3, mod(z - 2, NZ)), share(4, mod(z + 2, NZ))]
    for i, dy in ((1, -1), (2, 1), (3, 2)):
        for c in x_next[i - 1]:
            c.wait_recv()
        sends += x_next[i - 1]
        fars.append([rx(i, 2, block_of(dy, -1), first, x_up), rx(i, 3, block_of(dy, 1), second, x_dn)])
        if i == 1:
            for c in zs:
                c.wait_recv()
            sends += zs
            zs = zstep(3)
            cs += [share(5, mod(z - 3, NZ)), share(6, mod(z + 3, NZ))]
    for c in zs:
        c.wait_recv()
    sends += zs
    cs += [share(7, mod(z + 4, NZ))]
    for pair in fars:
        for c in pair:
            c.wait_recv()
        sends += pair
    for c in cs:
        c.wait()
    for c in sends:
        c.wait_send()

    acc[...] = jnp.zeros_like(acc)

    @pl.loop(0, NK)
    def _(kk):
        phase = lax.rem(kk, 4) * FB
        for f in range(FB):
            a = rg[kk, pl.ds(f * W, W), :].astype(jnp.float32)
            b = rg[kk, pl.ds(256 + f * W, W), :].astype(jnp.float32)
            cr, ci = tw_ref[phase + f], tw_ref[32 + phase + f]
            rg1[pl.ds(f * W, W), :] = (a * cr - b * ci).astype(jnp.bfloat16)
            rg1[pl.ds(256 + f * W, W), :] = (b * cr + a * ci).astype(jnp.bfloat16)

        @pl.loop(0, NZ)
        def _(zz):
            co, si = cosb[kk][None], sinb[kk][None]
            for j in range(4):
                chunk = sg[zz, j % 2, j // 2, kk].astype(jnp.float32)
                s0, s1_ = chunk[:8][:, None, :], chunk[8:][:, None, :]
                rows = pl.ds(j * 64, 64)
                lhs[rows, pl.ds(0, 256)] = (co * s0 + si * s1_).reshape(64, 256).astype(jnp.bfloat16)
                lhs[rows, pl.ds(256, 256)] = (co * s1_ - si * s0).reshape(64, 256).astype(jnp.bfloat16)
            left = lhs[...]
            acc[zz, 0] += jnp.dot(left, rg[kk], preferred_element_type=jnp.float32)
            acc[zz, 1] += jnp.dot(left, rg1[...], preferred_element_type=jnp.float32)

    @pl.loop(0, NZ)
    def _(zz):
        low = acc[zz, 0].reshape(32, 8, 256)
        high = acc[zz, 1].reshape(32, 8, 256)
        both = jnp.concatenate([low, high], axis=1) * (2.0 / F / W)
        out_ref[pl.ds(zz * 32, 32)] = both.astype(jnp.bfloat16)


def on_device(spectra, source_block):
    angles = np.arange(32) * (2.0 * math.pi / 32)
    table = jnp.asarray(np.concatenate([np.cos(angles), np.sin(angles)]).astype(np.float32))
    dma = pltpu.SemaphoreType.DMA
    bf = jnp.bfloat16
    return pl.pallas_call(
        kernel,
        out_shape=jax.ShapeDtypeStruct((256, LB, 256), bf),
        in_specs=[
            pl.BlockSpec(memory_space=pltpu.SMEM),
            pl.BlockSpec(memory_space=pltpu.SMEM),
            pl.BlockSpec(memory_space=pltpu.VMEM),
        ],
        out_specs=pl.BlockSpec(memory_space=pltpu.VMEM),
        scratch_shapes=[
            pltpu.VMEM((2, 2, W, 256), bf),
            pltpu.VMEM((4, NZ, 16, 256), bf),
            pltpu.VMEM((4, NZ, 16, 256), bf),
            pltpu.VMEM((NZ, 16, 256), bf),
            pltpu.VMEM((NZ, 16, 256), bf),
            pltpu.VMEM((NZ, NC, NYL, NK, 16, 256), bf),
            pltpu.VMEM((NK, 512, 256), bf),
            pltpu.VMEM((512, 256), bf),
            pltpu.VMEM((NK, 8, 256), jnp.float32),
            pltpu.VMEM((NK, 8, 256), jnp.float32),
            pltpu.VMEM((256, 512), bf),
            pltpu.VMEM((NZ, 2, 256, 256), jnp.float32),
            dma((2,)), dma((2,)),
            dma((4,)), dma((4,)),
            dma((8,)), dma((8,)),
            dma((4,)), dma((4,)),
            dma((8,)), dma((8,)),
            dma((2, 4)), dma((2, 4)),
            dma((8,)), dma((8,)),
            dma((4,)), dma((4,)),
            dma((4, 4)), dma((4, 4)),
        ],
        compiler_params=pltpu.CompilerParams(
            collective_id=0, has_side_effects=True, vmem_limit_bytes=40 * 2**20
        ),
        cost_estimate=pl.CostEstimate(flops=2 * 4096 * 8192 * 256, bytes_accessed=3 * 2**20, transcendentals=0),
    )(source_block, table, spectra)


def solution(mesh):
    in_specs = (P(None, "freq", None, "rx"), P())
    out_specs = P(None, "freq", "rx")
    return jax.shard_map(
        on_device, mesh=mesh, in_specs=in_specs, out_specs=out_specs, check_vma=False
    )
```

time: 392 us -> 122 us (0.31)
  waiting for transfers between devices: 293 us -> 0 us
  Pallas kernels: 0 us -> 117 us
  blocking collectives: 54.7 us -> 0 us
  between operations: 14.2 us -> 0.67 us
  starting transfers between devices: 13.3 us -> 0 us
  local copies, waits for them, and re-layouts: 9.73 us -> 2.92 us
  matrix products: 4 us -> 0 us
    psum x1 -> x0, waiting for transfers between devices: 238 us -> none  [broadcast(): return lax.psum(kept, axis)]
    pallas_call x0 -> x1, Pallas kernels: none -> 117 us  [on_device(): pl.pallas_call(kernel, out_shape=jax.ShapeDtypeStruct((256, LB, 256), bf)...]
    all_to_all x1 -> x0, blocking collectives: 54.7 us -> none  [on_device(): lax.all_to_all(lagged, 'freq', split_axis=1, concat_axis=0, tiled=True)]
    all_to_all x1 -> x0, waiting for transfers between devices: 52.8 us -> none  [on_device(): lax.all_to_all(cross, 'freq', split_axis=2, concat_axis=1, tiled=True)]
    all_to_all x1 -> x0, starting transfers between devices: 8.08 us -> none  [on_device(): lax.all_to_all(cross, 'freq', split_axis=2, concat_axis=1, tiled=True)]
    convert_element_type x2 -> x0, local copies, waits for them, and re-layouts: 5.83 us -> none  [the longest x1 3.34 us: transform(): return lagged.astype(jnp.bfloat16)]
    ppermute x2 -> x0, starting transfers between devices: 5.24 us -> none  [the longest x1 3.95 us: extended(): lax.ppermute(tail, axis, [(i, (i + 1) % count) for i in range(ends)])]
    dot_general x3 -> x0, matrix products: 4 us -> none  [the longest x1 3.04 us: transform(): jnp.einsum('kl,ksr->slr', basis_table, stacked, preferred_element_type=jn...]
  transfers between devices with their start and end apart: 4 -> 0, of which waited for: 3 -> 0; matrix products, arithmetic and copies ran while one was open for 0% -> 0% of each run, Pallas kernels for 0% -> 0%
where the time goes in v1:
time: 122 us; the launch traced here: 121 us
  Pallas kernels  117 us (96%)
  local copies, waits for them, and re-layouts  2.92 us (2%)
    pallas_call x1, Pallas kernels, on_device(): pl.pallas_call(kernel, out_shape=jax.ShapeDtypeStruct((256, LB, 256), bf)...  117 us
    unnamed x5, local copies, waits for them, and re-layouts  2.92 us

profile of v1, /device:TPU:1, one launch (start us, length us, event | category | flops | bytes accessed | tf_op | source)
XLA Modules:
  0.0 121.0 jit_solution(11958360974350131179)
XLA Ops:
  0.7 0.0 copy-start
  0.7 0.9 copy-done
  1.6 0.0 copy-start.1
  1.6 0.7 copy-done.1
  2.3 117.5 %shard_map.37 = bf16[256,16,256]{2,1,0:T(8,128)(2,1)S(1)} custom-call(s32[1]{0:T(128)S(6)} %copy.5.owner_ref, f32[64]{0:T(128)S(1)} %copy-done.1, bf16[2,8,32,256]{3,2,1,0:T(8,128)(2,1)S(1)} %copy-done), custom_call_target="tpu_custom_call" | custom-call | flops 17179869184 | bytes 3145728 | tf_op jit(solution)/shard_map/pallas_call | solution.py:249
  119.7 1.3 %copy.6 = bf16[256,16,256]{2,1,0:T(8,128)(2,1)} copy(bf16[256,16,256]{2,1,0:T(8,128)(2,1)S(1)} %shard_map.37) | data formatting | bytes 4194304
Async XLA Ops:
  0.7 1.0 copy-start
  1.6 0.7 copy-start.1

commit v2 on v1

v2 whole, which is shorter than its diff:
```python
import functools
import math

import jax
import jax.numpy as jnp
import numpy as np
from jax import lax
from jax.experimental import pallas as pl
from jax.experimental.pallas import tpu as pltpu
from jax.sharding import PartitionSpec as P

F = 128
W = 32
LAGS = 256
NX, NYH, NYL, NZ, NC = 4, 4, 2, 8, 2
NK = NX * NYH
FB = F // NK
LB = LAGS // NK
MESH = pl.DeviceIdType.MESH


def mod(a, n):
    return lax.rem(a + n, n)


def kernel(owner_ref, tw_ref, spec_ref, out_ref, halo, st_own, b1, b1s, b2, sg, rg, rg1, cosb, sinb, lhs, acc,
           halo_send, halo_recv, s1_send, s1_recv, s2_send, s2_recv, sx_send, sx_recv, sy_send, sy_recv,
           z_send, z_recv, c_send, c_recv, ry_send, ry_recv, rx_send, rx_recv):
    r = lax.axis_index("rx")
    k = lax.axis_index("freq")
    z = lax.div(r, 4)
    q = lax.rem(r, 4)
    yl = lax.div(q, 2)
    core = lax.rem(q, 2)
    yh = lax.div(k, 4)
    x = lax.rem(k, 4)

    def dev(z_, yl_, c_, yh_, x_):
        return (z_ * 4 + yl_ * 2 + c_, yh_ * 4 + x_)

    def remote(src, dst, send, recv, device):
        copy = pltpu.make_async_remote_copy(src, dst, send, recv, device_id=device, device_id_type=MESH)
        copy.start()
        return copy

    halo_peers = [(r, mod(k + 1, NK)), (r, mod(k - 1, NK))]
    q_peers = [(z * 4 + lax.rem(q + d, 4), k) for d in range(1, 4)]
    z_peers = [(lax.rem(z + d, NZ) * 4 + q, k) for d in range(1, NZ)]
    x_peers = [dev(z, yl, core, yh, lax.rem(x + d, NX)) for d in range(1, NX)]
    y = yh * 2 + yl
    y_peers = []
    for d in range(1, 8):
        yy = lax.rem(y + d, 8)
        y_peers.append(dev(z, lax.rem(yy, 2), core, lax.div(yy, 2), x))
    everyone = halo_peers + q_peers + z_peers + x_peers + y_peers

    barrier = pltpu.get_barrier_semaphore()
    for peer in everyone:
        pl.semaphore_signal(barrier, inc=1, device_id=peer, device_id_type=MESH)
    pl.semaphore_wait(barrier, len(everyone))

    up, down = halo_peers
    h0 = remote(spec_ref.at[:, FB - 1], halo.at[0], halo_send.at[0], halo_recv.at[0], up)
    h1 = remote(spec_ref.at[:, 0], halo.at[1], halo_send.at[1], halo_recv.at[1], down)

    lane = lax.broadcasted_iota(jnp.int32, (8, FB * W), 1)
    lag = lax.broadcasted_iota(jnp.int32, (8, FB * W), 0) + k * LB

    @pl.loop(0, NK)
    def _(kk):
        bins = kk * FB + lax.shift_right_logical(lane, 5)
        angle = jnp.bitwise_and(bins * lag, LAGS - 1).astype(jnp.float32) * (2.0 * math.pi / LAGS)
        cosb[kk] = jnp.cos(angle)
        sinb[kk] = jnp.sin(angle)

    h0.wait()
    h1.wait()

    def magnitude(a, b):
        return jnp.sqrt(a * a + b * b)

    lower = halo[0].astype(jnp.float32)
    upper = halo[1].astype(jnp.float32)
    m_low = jnp.where(k == 0, 0.0, magnitude(lower[0], lower[1]))
    m_high = jnp.where(k == NK - 1, 0.0, magnitude(upper[0], upper[1]))

    def raw(p, f):
        return spec_ref[p, f].astype(jnp.float32)

    mags = [m_low] + [magnitude(raw(0, f), raw(1, f)) for f in range(FB)] + [m_high]
    for f in range(FB):
        divisor = jnp.maximum((mags[f] + mags[f + 1] + mags[f + 2]) / 3.0, 0.5)
        for p in range(2):
            rg[k, pl.ds(p * 256 + f * W, W), :] = (raw(p, f) / divisor).astype(jnp.bfloat16)

    half = (pl.ds(0, 256), pl.ds(256, 256))
    y_to = (dev(z, yl, core, mod(yh + 1, NYH), x), dev(z, yl, core, mod(yh - 1, NYH), x))
    x_to = (dev(z, yl, core, yh, mod(x + 1, NX)), dev(z, yl, core, yh, mod(x - 1, NX)))
    sibling = dev(z, yl, 1 - core, yh, x)
    sends = []

    ring = jnp.where(core == 0, z, y)
    other = jnp.where(core == 0, y, z)

    def on_ring(a, b):
        zz, yy = jnp.where(core == 0, a, b), jnp.where(core == 0, b, a)
        return dev(zz, lax.rem(yy, 2), core, lax.div(yy, 2), x)

    ring_to = (on_ring(mod(ring + 1, 8), other), on_ring(mod(ring - 1, 8), other))

    def block_of(dyh, dx):
        return mod(yh + dyh, NYH) * NX + mod(x + dx, NX)

    def ry(way, slot, block, h):
        view = rg.at[block, half[h]]
        c = remote(view, view, ry_send.at[way, slot], ry_recv.at[way, slot], y_to[way])
        sends.append(c)
        return c

    def rx(row, way, slot, block, h):
        view = rg.at[block, half[h]]
        c = remote(view, view, rx_send.at[row, way, slot], rx_recv.at[row, way, slot], x_to[way])
        sends.append(c)
        return c

    def got(*copies):
        for c in copies:
            c.wait_recv()

    def xsend(row, block, h):
        return {(0, h): rx(row, 0, h, block, h), (1, h): rx(row, 1, h, block, h)}

    def rstep(t, u):
        pair = []
        for way in range(2):
            if t < 3 or way == u:
                view = sg.at[core, mod(ring - t, 8) if way == 0 else mod(ring + t, 8), pl.ds(u * 4, 4)]
                pair.append(remote(view, view, z_send.at[way, t, u], z_recv.at[way, t, u], ring_to[way]))
        sends.extend(pair)
        return pair

    cs = []

    def share(slot, a):
        view = sg.at[core, mod(ring + a, 8)]
        cs.append(remote(view, view, c_send.at[slot], c_recv.at[slot], sibling))

    for p in range(2):
        t = rg[k, pl.ds(p * 256, 256), :].astype(jnp.float32).T.reshape(NZ, 4, 8, FB * W)
        for j in range(4):
            st_own[j, :, pl.ds(p * 8, 8), :] = t[:, j].astype(jnp.bfloat16)
    s1 = [remote(st_own.at[lax.rem(q + d, 4)], b1.at[q], s1_send.at[d], s1_recv.at[d], q_peers[d - 1])
          for d in range(1, 4)]
    y0 = (ry(0, 0, k, 0), ry(1, 1, k, 1))
    x0 = {(0, 0): rx(0, 0, 0, k, 0), (1, 1): rx(0, 1, 1, k, 1)}
    y1 = (ry(0, 1, k, 1), ry(1, 0, k, 0))
    x0[0, 1] = rx(0, 0, 1, k, 1)
    x0[1, 0] = rx(0, 1, 0, k, 0)
    b1[q] = st_own[q]
    for c in s1:
        c.wait()
    owner = owner_ref[0]
    b1s[...] = b1[lax.rem(owner, 4)]
    s2 = [remote(b1s.at[lax.rem(z + d, NZ)], b2.at[z], s2_send.at[d], s2_recv.at[d], z_peers[d - 1])
          for d in range(1, NZ)]
    b2[z] = b1s[z]
    got(x0[0, 0], x0[1, 1])
    f0 = (rx(0, 0, 2, block_of(0, -1), 0), rx(0, 1, 2, block_of(0, 1), 1))
    for c in s2:
        c.wait()
    sg[core, ring, other, x] = b2[lax.div(owner, 4)]
    mine = sg.at[core, ring, other, x]
    sx = [remote(mine, mine, sx_send.at[d], sx_recv.at[d], x_peers[d - 1]) for d in range(1, NX)]
    got(*y0)
    y2 = (ry(0, 2, block_of(-1, 0), 0), ry(1, 2, block_of(1, 0), 1))
    x1 = xsend(1, block_of(-1, 0), 0)
    x2 = xsend(2, block_of(1, 0), 1)
    for c in sx:
        c.wait()
    srow = sg.at[core, ring, other]
    sy = [remote(srow, srow, sy_send.at[d], sy_recv.at[d], on_ring(ring, lax.rem(other + d, 8)))
          for d in range(1, 8)]
    got(*y1)
    x1.update(xsend(1, block_of(-1, 0), 1))
    x2.update(xsend(2, block_of(1, 0), 0))
    for c in sy:
        c.wait()
    ra, rb = rstep(0, 0), rstep(0, 1)
    share(0, 0)
    got(x1[0, 0], x2[1, 1])
    f1 = [rx(1, 0, 2, block_of(-1, -1), 0)]
    f2 = [rx(2, 1, 2, block_of(1, 1), 1)]
    got(*y2)
    x3 = xsend(3, block_of(2, 0), 0)
    x3.update(xsend(3, block_of(2, 0), 1))
    for t in range(1, 4):
        got(*ra)
        ra = rstep(t, 0)
        got(*rb)
        rb = rstep(t, 1)
        share(2 * t - 1, -t)
        share(2 * t, t)
        if t == 1:
            got(x1[1, 1], x2[0, 0])
            f1.append(rx(1, 1, 2, block_of(-1, 1), 1))
            f2.append(rx(2, 0, 2, block_of(1, -1), 0))
    got(*ra, *rb)
    share(7, 4)
    got(x3[0, 0], x3[1, 1])
    f3 = [rx(3, 0, 2, block_of(2, -1), 0), rx(3, 1, 2, block_of(2, 1), 1)]
    for c in cs:
        c.wait()
    def last():
        for c in sends:
            c.wait_send()

    def process(dy):
        row = mod(yh + dy, NYH)

        @pl.loop(0, 2)
        def _(pair):
            for i in range(2):
                xx = pair * 2 + i
                kk = row * NX + xx
                for f in range(FB):
                    a = rg[kk, pl.ds(f * W, W), :].astype(jnp.float32)
                    b = rg[kk, pl.ds(256 + f * W, W), :].astype(jnp.float32)
                    phase = lax.rem(kk, 4) * FB + f
                    cr, ci = tw_ref[phase], tw_ref[32 + phase]
                    rg1[pl.ds(i * 512 + f * W, W), :] = (a * cr - b * ci).astype(jnp.bfloat16)
                    rg1[pl.ds(i * 512 + 256 + f * W, W), :] = (b * cr + a * ci).astype(jnp.bfloat16)

                @pl.loop(0, NZ)
                def _(zz):
                    co, si = cosb[kk][None], sinb[kk][None]
                    for yl_ in range(2):
                        for c_ in range(2):
                            yy = row * 2 + yl_
                            chunk = (sg[0, zz, yy, xx] if c_ == 0 else sg[1, yy, zz, xx]).astype(jnp.float32)
                            s0, s1_ = chunk[:8][:, None, :], chunk[8:][:, None, :]
                            rows = pl.ds((yl_ * 2 + c_) * 64, 64)
                            lhs[zz, rows, pl.ds(i * 512, 256)] = (
                                (co * s0 + si * s1_).reshape(64, 256).astype(jnp.bfloat16))
                            lhs[zz, rows, pl.ds(i * 512 + 256, 256)] = (
                                (co * s1_ - si * s0).reshape(64, 256).astype(jnp.bfloat16))

            left = lhs[...].reshape(2048, 1024)
            right = rg[pl.ds(row * NX + pair * 2, 2)].reshape(1024, 256)
            acc[0] += jnp.dot(left, right, preferred_element_type=jnp.float32)
            acc[1] += jnp.dot(left, rg1[...], preferred_element_type=jnp.float32)

    acc[...] = jnp.zeros_like(acc)
    got(x0[0, 1], x0[1, 0], *f0)
    process(0)
    got(x1[0, 1], x1[1, 0], *f1)
    process(-1)
    got(x2[0, 1], x2[1, 0], *f2)
    process(1)
    got(x3[0, 1], x3[1, 0], *f3)
    process(2)
    last()

    @pl.loop(0, NZ)
    def _(zz):
        rows = pl.ds(zz * 256, 256)
        low = acc[0, rows, :].reshape(32, 8, 256)
        high = acc[1, rows, :].reshape(32, 8, 256)
        both = jnp.concatenate([low, high], axis=1) * (2.0 / F / W)
        out_ref[pl.ds(zz * 32, 32)] = both.astype(jnp.bfloat16)


def on_device(spectra, source_block):
    angles = np.arange(32) * (2.0 * math.pi / 32)
    table = jnp.asarray(np.concatenate([np.cos(angles), np.sin(angles)]).astype(np.float32))
    dma = pltpu.SemaphoreType.DMA
    bf = jnp.bfloat16
    return pl.pallas_call(
        kernel,
        out_shape=jax.ShapeDtypeStruct((256, LB, 256), bf),
        in_specs=[
            pl.BlockSpec(memory_space=pltpu.SMEM),
            pl.BlockSpec(memory_space=pltpu.SMEM),
            pl.BlockSpec(memory_space=pltpu.VMEM),
        ],
        out_specs=pl.BlockSpec(memory_space=pltpu.VMEM),
        scratch_shapes=[
            pltpu.VMEM((2, 2, W, 256), bf),
            pltpu.VMEM((4, NZ, 16, 256), bf),
            pltpu.VMEM((4, NZ, 16, 256), bf),
            pltpu.VMEM((NZ, 16, 256), bf),
            pltpu.VMEM((NZ, 16, 256), bf),
            pltpu.VMEM((NC, 8, 8, NX, 16, 256), bf),
            pltpu.VMEM((NK, 512, 256), bf),
            pltpu.VMEM((1024, 256), bf),
            pltpu.VMEM((NK, 8, 256), jnp.float32),
            pltpu.VMEM((NK, 8, 256), jnp.float32),
            pltpu.VMEM((NZ, 256, 1024), bf),
            pltpu.VMEM((2, 2048, 256), jnp.float32),
            dma((2,)), dma((2,)),
            dma((4,)), dma((4,)),
            dma((8,)), dma((8,)),
            dma((4,)), dma((4,)),
            dma((8,)), dma((8,)),
            dma((2, 4, 2)), dma((2, 4, 2)),
            dma((8,)), dma((8,)),
            dma((2, 3)), dma((2, 3)),
            dma((4, 2, 3)), dma((4, 2, 3)),
        ],
        compiler_params=pltpu.CompilerParams(
            collective_id=0, has_side_effects=True, vmem_limit_bytes=48 * 2**20
        ),
        cost_estimate=pl.CostEstimate(flops=2 * 4096 * 8192 * 256, bytes_accessed=3 * 2**20, transcendentals=0),
    )(source_block, table, spectra)


def solution(mesh):
    in_specs = (P(None, "freq", None, "rx"), P())
    out_specs = P(None, "freq", "rx")
    return jax.shard_map(
        on_device, mesh=mesh, in_specs=in_specs, out_specs=out_specs, check_vma=False
    )
```

time: 122 us -> 106 us (0.87)
  Pallas kernels: 117 us -> 102 us
    pallas_call x1, Pallas kernels: 117 us -> 102 us  [on_device(): pl.pallas_call(kernel, out_shape=jax.ShapeDtypeStruct((256, LB, 256), bf)...]
where the time goes in v2:
time: 106 us; the launch traced here: 105 us
  Pallas kernels  102 us (96%)
  local copies, waits for them, and re-layouts  2.92 us (3%)
    pallas_call x1, Pallas kernels, on_device(): pl.pallas_call(kernel, out_shape=jax.ShapeDtypeStruct((256, LB, 256), bf)...  102 us
    unnamed x5, local copies, waits for them, and re-layouts  2.92 us

profile of v2, /device:TPU:1, one launch (start us, length us, event | category | flops | bytes accessed | tf_op | source)
XLA Modules:
  0.0 105.4 jit_solution(3780122208668201124)
XLA Ops:
  0.7 0.0 copy-start
  0.7 0.9 copy-done
  1.6 0.0 copy-start.1
  1.6 0.7 copy-done.1
  2.3 101.8 %shard_map.37 = bf16[256,16,256]{2,1,0:T(8,128)(2,1)S(1)} custom-call(s32[1]{0:T(128)S(6)} %copy.5.owner_ref, f32[64]{0:T(128)S(1)} %copy-done.1, bf16[2,8,32,256]{3,2,1,0:T(8,128)(2,1)S(1)} %copy-done), custom_call_target="tpu_custom_call" | custom-call | flops 17179869184 | bytes 3145728 | tf_op jit(solution)/shard_map/pallas_call | solution.py:277
  104.1 1.3 %copy.6 = bf16[256,16,256]{2,1,0:T(8,128)(2,1)} copy(bf16[256,16,256]{2,1,0:T(8,128)(2,1)S(1)} %shard_map.37) | data formatting | bytes 4194304
Async XLA Ops:
  0.7 1.0 copy-start
  1.6 0.7 copy-start.1

commit v3 on v2

v3 whole, which is shorter than its diff:
```python
import math

import jax
import jax.numpy as jnp
from jax import lax
from jax.experimental import pallas as pl
from jax.experimental.pallas import tpu as pltpu
from jax.sharding import PartitionSpec as P

F = 128
W = 32
LAGS = 256
NX, NYH, NYL, NZ, NC = 4, 4, 2, 8, 2
NK = NX * NYH
FB = F // NK
LB = LAGS // NK
MESH = pl.DeviceIdType.MESH


def mod(a, n):
    return lax.rem(a + n, n)


def kernel(owner_ref, spec_hbm, out_ref, spec_ref, halo, st_own, b1, b1s, b2, sg, rg, rg1, cosb, sinb, lhs, acc, turned,
           spec_sem, halo_send, halo_recv, s1_send, s1_recv, s2_send, s2_recv, sx_send, sx_recv, sy_send, sy_recv,
           z_send, z_recv, c_send, c_recv, ry_send, ry_recv, rx_send, rx_recv):
    r = lax.axis_index("rx")
    k = lax.axis_index("freq")
    z = lax.div(r, 4)
    q = lax.rem(r, 4)
    yl = lax.div(q, 2)
    core = lax.rem(q, 2)
    yh = lax.div(k, 4)
    x = lax.rem(k, 4)

    def dev(z_, yl_, c_, yh_, x_):
        return (z_ * 4 + yl_ * 2 + c_, yh_ * 4 + x_)

    def remote(src, dst, send, recv, device):
        copy = pltpu.make_async_remote_copy(src, dst, send, recv, device_id=device, device_id_type=MESH)
        copy.start()
        return copy

    halo_peers = [(r, mod(k + 1, NK)), (r, mod(k - 1, NK))]
    q_peers = [(z * 4 + lax.rem(q + d, 4), k) for d in range(1, 4)]
    z_peers = [(lax.rem(z + d, NZ) * 4 + q, k) for d in range(1, NZ)]
    x_peers = [dev(z, yl, core, yh, lax.rem(x + d, NX)) for d in range(1, NX)]
    y = yh * 2 + yl
    y_peers = []
    for d in range(1, 8):
        yy = lax.rem(y + d, 8)
        y_peers.append(dev(z, lax.rem(yy, 2), core, lax.div(yy, 2), x))
    everyone = halo_peers + q_peers + z_peers + x_peers + y_peers

    fetch = pltpu.make_async_copy(spec_hbm, spec_ref, spec_sem.at[0])
    fetch.start()
    barrier = pltpu.get_barrier_semaphore()
    for peer in everyone:
        pl.semaphore_signal(barrier, inc=1, device_id=peer, device_id_type=MESH)
    pl.semaphore_wait(barrier, len(everyone))

    up, down = halo_peers
    h0 = remote(spec_hbm.at[:, FB - 1], halo.at[0], halo_send.at[0], halo_recv.at[0], up)
    h1 = remote(spec_hbm.at[:, 0], halo.at[1], halo_send.at[1], halo_recv.at[1], down)

    lane = lax.broadcasted_iota(jnp.int32, (8, FB * W), 1)
    lag = lax.broadcasted_iota(jnp.int32, (8, FB * W), 0) + k * LB

    @pl.loop(0, NK)
    def _(kk):
        bins = kk * FB + lax.shift_right_logical(lane, 5)
        angle = jnp.bitwise_and(bins * lag, LAGS - 1).astype(jnp.float32) * (2.0 * math.pi / LAGS)
        for table, values in ((cosb, jnp.cos(angle)), (sinb, jnp.sin(angle))):
            for c in range(2):
                for lc in range(8):
                    line = values[lc:lc + 1, c * 128:(c + 1) * 128]
                    table[kk, c, lc] = jnp.broadcast_to(line, (16, 128)).astype(jnp.bfloat16)

    fetch.wait()
    acc[...] = jnp.zeros_like(acc)
    h0.wait()
    h1.wait()

    def magnitude(a, b):
        return jnp.sqrt(a * a + b * b)

    lower = halo[0].astype(jnp.float32)
    upper = halo[1].astype(jnp.float32)
    m_low = jnp.where(k == 0, 0.0, magnitude(lower[0], lower[1]))
    m_high = jnp.where(k == NK - 1, 0.0, magnitude(upper[0], upper[1]))

    def raw(p, f):
        return spec_ref[p, f].astype(jnp.float32)

    mags = [m_low] + [magnitude(raw(0, f), raw(1, f)) for f in range(FB)] + [m_high]
    for f in range(FB):
        divisor = jnp.maximum((mags[f] + mags[f + 1] + mags[f + 2]) / 3.0, 0.5)
        for p in range(2):
            rg[k, pl.ds(f // 4 * 256 + p * 128 + f % 4 * W, W), :] = (raw(p, f) / divisor).astype(jnp.bfloat16)

    half = (pl.ds(0, 256), pl.ds(256, 256))
    y_to = (dev(z, yl, core, mod(yh + 1, NYH), x), dev(z, yl, core, mod(yh - 1, NYH), x))
    x_to = (dev(z, yl, core, yh, mod(x + 1, NX)), dev(z, yl, core, yh, mod(x - 1, NX)))
    sibling = dev(z, yl, 1 - core, yh, x)
    sends = []

    ring = jnp.where(core == 0, z, y)
    other = jnp.where(core == 0, y, z)

    def on_ring(a, b):
        zz, yy = jnp.where(core == 0, a, b), jnp.where(core == 0, b, a)
        return dev(zz, lax.rem(yy, 2), core, lax.div(yy, 2), x)

    ring_to = (on_ring(mod(ring + 1, 8), other), on_ring(mod(ring - 1, 8), other))

    def block_of(dyh, dx):
        return mod(yh + dyh, NYH) * NX + mod(x + dx, NX)

    def launch(make):
        make().start()
        sends.append(make)
        return make

    def ry(way, slot, block, h):
        def make():
            view = rg.at[block_of(*block), half[h]]
            return pltpu.make_async_remote_copy(view, view, ry_send.at[way, slot], ry_recv.at[way, slot],
                                                device_id=y_to[way], device_id_type=MESH)

        return launch(make)

    def rx(row, way, slot, block, h):
        def make():
            view = rg.at[block_of(*block), half[h]]
            return pltpu.make_async_remote_copy(view, view, rx_send.at[row, way, slot], rx_recv.at[row, way, slot],
                                                device_id=x_to[way], device_id_type=MESH)

        return launch(make)

    def got(*copies):
        for c in copies:
            (c() if callable(c) else c).wait_recv()

    def xsend(row, block, h):
        return {(0, h): rx(row, 0, h, block, h), (1, h): rx(row, 1, h, block, h)}

    def rpart(t, u, way):
        def make():
            view = sg.at[core, mod(ring - t, 8) if way == 0 else mod(ring + t, 8), pl.ds(u * 4, 4)]
            return pltpu.make_async_remote_copy(view, view, z_send.at[way, t, u], z_recv.at[way, t, u],
                                                device_id=ring_to[way], device_id_type=MESH)

        return launch(make)

    def rstep(t, u):
        return [rpart(t, u, way) for way in range(2) if t < 3 or way == u]

    cs = []

    def share(slot, a):
        def make():
            view = sg.at[core, mod(ring + a, 8)]
            return pltpu.make_async_remote_copy(view, view, c_send.at[slot], c_recv.at[slot],
                                                device_id=sibling, device_id_type=MESH)

        cs.append(launch(make))

    def build(c, a):
        @pl.loop(0, 8)
        def _(b):
            zz, yy = jnp.where(c == 0, a, b), jnp.where(c == 0, b, a)
            row, yl_ = lax.div(yy, 2), lax.rem(yy, 2)
            for xx in range(NX):
                kk = row * NX + xx
                s0, s1_ = sg[c, a, b, xx, 0], sg[c, a, b, xx, 1]
                for lc in range(8):
                    co, si = cosb[kk, c, lc], sinb[kk, c, lc]
                    rows = pl.ds(pl.multiple_of(zz * 256 + lc * 32 + yl_ * 16, 16), 16)
                    lhs[c, row, rows, pl.ds(xx * 256, 128)] = co * s0 + si * s1_
                    lhs[c, row, rows, pl.ds(xx * 256 + 128, 128)] = co * s1_ - si * s0

    def process(c, row):
        for xx in range(NX):
            kk = row * NX + xx
            for g in range(4):
                angles = [2.0 * math.pi / 32 * (xx * FB + m * 4 + g) for m in range(2)]
                cr = jnp.where(c == 0, math.cos(angles[0]), math.cos(angles[1]))
                ci = jnp.where(c == 0, math.sin(angles[0]), math.sin(angles[1]))
                a = rg[kk, pl.ds(pl.multiple_of(c * 256 + g * W, W), W), :].astype(jnp.float32)
                b = rg[kk, pl.ds(pl.multiple_of(c * 256 + 128 + g * W, W), W), :].astype(jnp.float32)
                rg1[pl.ds(xx * 256 + g * W, W), :] = (a * cr - b * ci).astype(jnp.bfloat16)
                rg1[pl.ds(xx * 256 + 128 + g * W, W), :] = (b * cr + a * ci).astype(jnp.bfloat16)
        left = lhs[c, row]
        right = rg[pl.ds(row * NX, NX), pl.ds(pl.multiple_of(c * 256, 256), 256), :].reshape(1024, 256)
        acc[0] += jnp.dot(left, right, preferred_element_type=jnp.float32)
        acc[1] += jnp.dot(left, rg1[...], preferred_element_type=jnp.float32)

    for p in range(2):
        for c in range(2):
            t = rg[k, pl.ds(c * 256 + p * 128, 128), :].astype(jnp.float32).T.astype(jnp.bfloat16)
            t = t.reshape(NZ, 2, 16, 128)
            for yl_ in range(2):
                st_own[yl_ * 2 + c, :, p] = t[:, yl_]
    s1 = [remote(st_own.at[lax.rem(q + d, 4)], b1.at[q], s1_send.at[d], s1_recv.at[d], q_peers[d - 1])
          for d in range(1, 4)]
    T = {}
    plan = dict(y0=0, y1=0, g0=2, y2=3, g1=3, fa=3, fb=4, g2=6, f3=7)

    def at(point):
        for name, step in events:
            if plan[name] == point:
                step()

    def y0():
        T["y0"] = (ry(0, 0, (0, 0), 0), ry(1, 1, (0, 0), 1))

    def y1():
        T["y1"] = (ry(0, 1, (0, 0), 1), ry(1, 0, (0, 0), 0))

    def g0():
        got(*T["y0"])
        T["x1"] = xsend(1, (-1, 0), 0)
        T["x2"] = xsend(2, (1, 0), 1)

    def y2():
        T["y2"] = (ry(0, 2, (-1, 0), 0), ry(1, 2, (1, 0), 1))

    def g1():
        got(*T["y1"])
        T["x1"].update(xsend(1, (-1, 0), 1))
        T["x2"].update(xsend(2, (1, 0), 0))

    def fa():
        got(T["x1"][0, 0], T["x2"][1, 1])
        T["f1"] = [rx(1, 0, 2, (-1, -1), 0)]
        T["f2"] = [rx(2, 1, 2, (1, 1), 1)]

    def fb():
        got(T["x1"][1, 1], T["x2"][0, 0])
        T["f1"].append(rx(1, 1, 2, (-1, 1), 1))
        T["f2"].append(rx(2, 0, 2, (1, -1), 0))

    def g2():
        got(*T["y2"])
        T["x3"] = xsend(3, (2, 0), 0)
        T["x3"].update(xsend(3, (2, 0), 1))

    def f3():
        got(T["x3"][0, 0], T["x3"][1, 1])
        T["f3"] = [rx(3, 0, 2, (2, -1), 0), rx(3, 1, 2, (2, 1), 1)]

    events = [("y0", y0), ("y1", y1), ("g0", g0), ("y2", y2), ("g1", g1), ("fa", fa), ("fb", fb), ("g2", g2), ("f3", f3)]

    at(0)
    x0 = {(0, 0): rx(0, 0, 0, (0, 0), 0), (1, 1): rx(0, 1, 1, (0, 0), 1)}
    x0[0, 1] = rx(0, 0, 1, (0, 0), 1)
    x0[1, 0] = rx(0, 1, 0, (0, 0), 0)
    b1[q] = st_own[q]
    got(*s1)
    sends.extend(s1)
    owner = owner_ref[0]
    b1s[...] = b1[lax.rem(owner, 4)]
    s2 = [remote(b1s.at[lax.rem(z + d, NZ)], b2.at[z], s2_send.at[d], s2_recv.at[d], z_peers[d - 1])
          for d in range(1, NZ)]
    b2[z] = b1s[z]
    at(1)
    got(x0[0, 0], x0[1, 1])
    f0 = (rx(0, 0, 2, (0, -1), 0), rx(0, 1, 2, (0, 1), 1))
    got(*s2)
    sends.extend(s2)
    sg[core, ring, other, x] = b2[lax.div(owner, 4)]
    mine = sg.at[core, ring, other, x]
    sx = [remote(mine, mine, sx_send.at[d], sx_recv.at[d], x_peers[d - 1]) for d in range(1, NX)]
    got(*sx)
    sends.extend(sx)
    srow = sg.at[core, ring, other]
    sy = [remote(srow, srow, sy_send.at[d], sy_recv.at[d], on_ring(ring, lax.rem(other + d, 8)))
          for d in range(1, 8)]
    at(2)
    got(*sy)
    sends.extend(sy)
    ra = rstep(0, 0)
    for c in ra:
        c().wait_send()
    del sends[-2:]
    rb = rstep(0, 1)
    share(0, 0)
    at(3)
    build(core, ring)
    def advance(t):
        T["ra"], old = None, T["ra"]
        got(*old)
        T["ra"] = rstep(t, 0)
        got(*T["rb"])
        T["rb"] = rstep(t, 1)
        share(2 * t - 1, -t)
        share(2 * t, t)
        at(3 + t)
        build(core, mod(ring - t, 8))
        build(core, mod(ring + t, 8))
        for slot in ((0,) if t == 1 else (2 * t - 3, 2 * t - 2)):
            got(cs[slot])
            build(1 - core, mod(other + (-(t - 1) if slot % 2 else t - 1), 8))

    T["ra"], T["rb"] = ra, rb
    advance(1)
    advance(2)
    got(x0[0, 1], x0[1, 0], *f0)

    @pl.loop(0, 8)
    def _(item):
        @pl.when(item == 1)
        def _():
            advance(3)
            got(*T["ra"], *T["rb"])
            share(7, 4)
            at(7)
            build(core, mod(ring + 4, 8))
            for slot, d in ((5, -3), (6, 3), (7, 4)):
                got(cs[slot])
                build(1 - core, mod(other + d, 8))

        @pl.when(item == 2)
        def _():
            at(8)
            got(T["x1"][0, 1], T["x1"][1, 0], *T["f1"])

        @pl.when(item == 4)
        def _():
            at(9)
            got(T["x2"][0, 1], T["x2"][1, 0], *T["f2"])

        @pl.when(item == 6)
        def _():
            at(10)
            got(T["x3"][0, 1], T["x3"][1, 0], *T["f3"])

        c = jnp.where(item < 2, 1 - item, lax.rem(item, 2))
        dy = jnp.where(item < 2, 0, jnp.where(item < 4, 3, jnp.where(item < 6, 1, 2)))
        process(c, lax.rem(yh + dy, NYH))

    for c in sends:
        (c() if callable(c) else c).wait_send()

    @pl.loop(0, NZ)
    def _(zz):
        for n in range(2):
            lanes = pl.ds(n * 128, 128)
            for lf in range(2):
                for lc in range(8):
                    turned[n, pl.ds(lf * 8 + lc, 32, stride=16), :] = acc[lf, pl.ds(zz * 256 + lc * 32, 32), lanes]
            both = turned[n].reshape(32, LB, 128) * (2.0 / F / W)
            out_ref[pl.ds(zz * 32, 32), :, lanes] = both.astype(jnp.bfloat16)


def on_device(spectra, source_block):
    dma = pltpu.SemaphoreType.DMA
    bf = jnp.bfloat16
    return pl.pallas_call(
        kernel,
        out_shape=jax.ShapeDtypeStruct((256, LB, 256), bf),
        in_specs=[
            pl.BlockSpec(memory_space=pltpu.SMEM),
            pl.BlockSpec(memory_space=pl.ANY),
        ],
        out_specs=pl.BlockSpec(memory_space=pltpu.VMEM),
        scratch_shapes=[
            pltpu.VMEM((2, FB, W, 256), bf),
            pltpu.VMEM((2, 2, W, 256), bf),
            pltpu.VMEM((4, NZ, 2, 16, 128), bf),
            pltpu.VMEM((4, NZ, 2, 16, 128), bf),
            pltpu.VMEM((NZ, 2, 16, 128), bf),
            pltpu.VMEM((NZ, 2, 16, 128), bf),
            pltpu.VMEM((NC, 8, 8, NX, 2, 16, 128), bf),
            pltpu.VMEM((NK, 512, 256), bf),
            pltpu.VMEM((1024, 256), bf),
            pltpu.VMEM((NK, 2, 8, 16, 128), bf),
            pltpu.VMEM((NK, 2, 8, 16, 128), bf),
            pltpu.VMEM((NC, NYH, 2048, 1024), bf),
            pltpu.VMEM((2, 2048, 256), jnp.float32),
            pltpu.VMEM((2, 512, 128), jnp.float32),
            dma((1,)),
            dma((2,)), dma((2,)),
            dma((4,)), dma((4,)),
            dma((8,)), dma((8,)),
            dma((4,)), dma((4,)),
            dma((8,)), dma((8,)),
            dma((2, 4, 2)), dma((2, 4, 2)),
            dma((8,)), dma((8,)),
            dma((2, 3)), dma((2, 3)),
            dma((4, 2, 3)), dma((4, 2, 3)),
        ],
        compiler_params=pltpu.CompilerParams(
            collective_id=0, has_side_effects=True, vmem_limit_bytes=56 * 2**20
        ),
        cost_estimate=pl.CostEstimate(flops=2 * 4096 * 8192 * 256, bytes_accessed=3 * 2**20, transcendentals=0),
    )(source_block, spectra)


def solution(mesh):
    in_specs = (P(None, "freq", None, "rx"), P())
    out_specs = P(None, "freq", "rx")
    return jax.shard_map(
        on_device, mesh=mesh, in_specs=in_specs, out_specs=out_specs, check_vma=False
    )
```

time: 106 us -> 98 us (0.925)
  Pallas kernels: 102 us -> 92.6 us
    pallas_call x1, Pallas kernels: 102 us -> 92.6 us  [on_device(): pl.pallas_call(kernel, out_shape=jax.ShapeDtypeStruct((256, LB, 256), bf)...]
    unnamed x5 -> x1, local copies, waits for them, and re-layouts: 2.92 us -> 3.05 us
where the time goes in v3:
time: 98 us; the launch traced here: 96.4 us
  Pallas kernels  92.6 us (94%)
  local copies, waits for them, and re-layouts  3.05 us (3%)
    pallas_call x1, Pallas kernels, on_device(): pl.pallas_call(kernel, out_shape=jax.ShapeDtypeStruct((256, LB, 256), bf)...  92.6 us
    unnamed x1, local copies, waits for them, and re-layouts  3.05 us

profile of v3, /device:TPU:1, one launch (start us, length us, event | category | flops | bytes accessed | tf_op | source)
XLA Modules:
  0.0 96.4 jit_solution(12660732446943111099)
XLA Ops:
  0.7 92.6 %shard_map.28 = bf16[256,16,256]{2,1,0:T(8,128)(2,1)} custom-call(s32[1]{0:T(128)S(6)} %copy.4.owner_ref, bf16[2,8,32,256]{3,2,1,0:T(8,128)(2,1)} %spec_hbm.1), custom_call_target="tpu_custom_call" | custom-call | flops 17179869184 | bytes 3145728 | tf_op jit(solution)/shard_map/pallas_call | solution.py:359
  93.3 3.0 %copy.5 = bf16[256,16,256]{2,1,0:T(8,128)(2,1)} copy(bf16[256,16,256]{2,1,0:T(8,128)(2,1)} %shard_map.28) | data formatting | bytes 4194304

commit v4 on v3

--- a/solution.py
+++ b/solution.py
@@ -21,8 +21,8 @@
     return lax.rem(a + n, n)
 
 
-def kernel(owner_ref, spec_hbm, out_ref, spec_ref, halo, st_own, b1, b1s, b2, sg, rg, rg1, cosb, sinb, lhs, acc, turned,
-           spec_sem, halo_send, halo_recv, s1_send, s1_recv, s2_send, s2_recv, sx_send, sx_recv, sy_send, sy_recv,
+def kernel(owner_ref, spec_hbm, out_ref, spec_ref, halo, st_own, b2, sg, rg, rg1, cosb, sinb, lhs, acc, turned,
+           spec_sem, halo_send, halo_recv, s1_send, s1_recv, sx_send, sx_recv,
            z_send, z_recv, c_send, c_recv, ry_send, ry_recv, rx_send, rx_recv):
     r = lax.axis_index("rx")
     k = lax.axis_index("freq")
@@ -42,22 +42,42 @@
         return copy
 
     halo_peers = [(r, mod(k + 1, NK)), (r, mod(k - 1, NK))]
-    q_peers = [(z * 4 + lax.rem(q + d, 4), k) for d in range(1, 4)]
-    z_peers = [(lax.rem(z + d, NZ) * 4 + q, k) for d in range(1, NZ)]
-    x_peers = [dev(z, yl, core, yh, lax.rem(x + d, NX)) for d in range(1, NX)]
     y = yh * 2 + yl
-    y_peers = []
-    for d in range(1, 8):
-        yy = lax.rem(y + d, 8)
-        y_peers.append(dev(z, lax.rem(yy, 2), core, lax.div(yy, 2), x))
-    everyone = halo_peers + q_peers + z_peers + x_peers + y_peers
+
+    ring = jnp.where(core == 0, z, y)
+    other = jnp.where(core == 0, y, z)
+    place = other * NX + x
+
+    def on_ring(a, b, x_):
+        zz, yy = jnp.where(core == 0, a, b), jnp.where(core == 0, b, a)
+        return dev(zz, lax.rem(yy, 2), core, lax.div(yy, 2), x_)
+
+    ring_to = (on_ring(mod(ring + 1, 8), other, x), on_ring(mod(ring - 1, 8), other, x))
+
+    def rx_peer(d):
+        return (lax.rem(r + d, 32), k)
+
+    def plane_peer(d):
+        n = lax.rem(place + d, 32)
+        return on_ring(ring, lax.div(n, NX), lax.rem(n, NX))
+
+    y_to = (dev(z, yl, core, mod(yh + 1, NYH), x), dev(z, yl, core, mod(yh - 1, NYH), x))
+    x_to = (dev(z, yl, core, yh, mod(x + 1, NX)), dev(z, yl, core, yh, mod(x - 1, NX)))
+    sibling = dev(z, yl, 1 - core, yh, x)
+    near = halo_peers + list(ring_to) + list(y_to)
 
     fetch = pltpu.make_async_copy(spec_hbm, spec_ref, spec_sem.at[0])
     fetch.start()
     barrier = pltpu.get_barrier_semaphore()
-    for peer in everyone:
+    for peer in near:
         pl.semaphore_signal(barrier, inc=1, device_id=peer, device_id_type=MESH)
-    pl.semaphore_wait(barrier, len(everyone))
+
+    @pl.loop(1, 32)
+    def _(d):
+        pl.semaphore_signal(barrier, inc=1, device_id=rx_peer(d), device_id_type=MESH)
+        pl.semaphore_signal(barrier, inc=1, device_id=plane_peer(d), device_id_type=MESH)
+
+    pl.semaphore_wait(barrier, len(near) + 62)
 
     up, down = halo_peers
     h0 = remote(spec_hbm.at[:, FB - 1], halo.at[0], halo_send.at[0], halo_recv.at[0], up)
@@ -99,19 +119,7 @@
             rg[k, pl.ds(f // 4 * 256 + p * 128 + f % 4 * W, W), :] = (raw(p, f) / divisor).astype(jnp.bfloat16)
 
     half = (pl.ds(0, 256), pl.ds(256, 256))
-    y_to = (dev(z, yl, core, mod(yh + 1, NYH), x), dev(z, yl, core, mod(yh - 1, NYH), x))
-    x_to = (dev(z, yl, core, yh, mod(x + 1, NX)), dev(z, yl, core, yh, mod(x - 1, NX)))
-    sibling = dev(z, yl, 1 - core, yh, x)
     sends = []
-
-    ring = jnp.where(core == 0, z, y)
-    other = jnp.where(core == 0, y, z)
-
-    def on_ring(a, b):
-        zz, yy = jnp.where(core == 0, a, b), jnp.where(core == 0, b, a)
-        return dev(zz, lax.rem(yy, 2), core, lax.div(yy, 2), x)
-
-    ring_to = (on_ring(mod(ring + 1, 8), other), on_ring(mod(ring - 1, 8), other))
 
     def block_of(dyh, dx):
         return mod(yh + dyh, NYH) * NX + mod(x + dx, NX)
@@ -200,11 +208,24 @@
             t = rg[k, pl.ds(c * 256 + p * 128, 128), :].astype(jnp.float32).T.astype(jnp.bfloat16)
             t = t.reshape(NZ, 2, 16, 128)
             for yl_ in range(2):
-                st_own[yl_ * 2 + c, :, p] = t[:, yl_]
-    s1 = [remote(st_own.at[lax.rem(q + d, 4)], b1.at[q], s1_send.at[d], s1_recv.at[d], q_peers[d - 1])
-          for d in range(1, 4)]
+                st_own[:, yl_ * 2 + c, p] = t[:, yl_]
+
+    def exchange(d):
+        j = lax.rem(r + d, 32)
+        return pltpu.make_async_remote_copy(st_own.at[lax.div(j, 4), lax.rem(j, 4)], b2.at[r], s1_send.at[d],
+                                            s1_recv.at[d], device_id=rx_peer(d), device_id_type=MESH)
+
+    def spread(d):
+        view = sg.at[core, ring, other, x]
+        return pltpu.make_async_remote_copy(view, view, sx_send.at[d], sx_recv.at[d],
+                                            device_id=plane_peer(d), device_id_type=MESH)
+
+    @pl.loop(1, 32)
+    def _(d):
+        exchange(d).start()
+
     T = {}
-    plan = dict(y0=0, y1=0, g0=2, y2=3, g1=3, fa=3, fb=4, g2=6, f3=7)
+    plan = dict(y0=1, y1=3, g0=2, y2=5, g1=4, fa=4, fb=5, g2=7, f3=8)
 
     def at(point):
         for name, step in events:
@@ -255,30 +276,28 @@
     x0 = {(0, 0): rx(0, 0, 0, (0, 0), 0), (1, 1): rx(0, 1, 1, (0, 0), 1)}
     x0[0, 1] = rx(0, 0, 1, (0, 0), 1)
     x0[1, 0] = rx(0, 1, 0, (0, 0), 0)
-    b1[q] = st_own[q]
-    got(*s1)
-    sends.extend(s1)
+    b2[r] = st_own[z, q]
     owner = owner_ref[0]
-    b1s[...] = b1[lax.rem(owner, 4)]
-    s2 = [remote(b1s.at[lax.rem(z + d, NZ)], b2.at[z], s2_send.at[d], s2_recv.at[d], z_peers[d - 1])
-          for d in range(1, NZ)]
-    b2[z] = b1s[z]
-    at(1)
     got(x0[0, 0], x0[1, 1])
     f0 = (rx(0, 0, 2, (0, -1), 0), rx(0, 1, 2, (0, 1), 1))
-    got(*s2)
-    sends.extend(s2)
-    sg[core, ring, other, x] = b2[lax.div(owner, 4)]
-    mine = sg.at[core, ring, other, x]
-    sx = [remote(mine, mine, sx_send.at[d], sx_recv.at[d], x_peers[d - 1]) for d in range(1, NX)]
-    got(*sx)
-    sends.extend(sx)
-    srow = sg.at[core, ring, other]
-    sy = [remote(srow, srow, sy_send.at[d], sy_recv.at[d], on_ring(ring, lax.rem(other + d, 8)))
-          for d in range(1, 8)]
+
+    @pl.loop(1, 32)
+    def _(d):
+        exchange(d).wait_recv()
+
+    sg[core, ring, other, x] = b2[owner]
+
+    @pl.loop(1, 32)
+    def _(d):
+        spread(d).start()
+
+    at(1)
     at(2)
-    got(*sy)
-    sends.extend(sy)
+
+    @pl.loop(1, 32)
+    def _(d):
+        spread(d).wait_recv()
+
     ra = rstep(0, 0)
     for c in ra:
         c().wait_send()
@@ -339,6 +358,11 @@
         dy = jnp.where(item < 2, 0, jnp.where(item < 4, 3, jnp.where(item < 6, 1, 2)))
         process(c, lax.rem(yh + dy, NYH))
 
+    @pl.loop(1, 32)
+    def _(d):
+        exchange(d).wait_send()
+        spread(d).wait_send()
+
     for c in sends:
         (c() if callable(c) else c).wait_send()
 
@@ -367,10 +391,8 @@
         scratch_shapes=[
             pltpu.VMEM((2, FB, W, 256), bf),
             pltpu.VMEM((2, 2, W, 256), bf),
-            pltpu.VMEM((4, NZ, 2, 16, 128), bf),
-            pltpu.VMEM((4, NZ, 2, 16, 128), bf),
-            pltpu.VMEM((NZ, 2, 16, 128), bf),
-            pltpu.VMEM((NZ, 2, 16, 128), bf),
+            pltpu.VMEM((NZ, 4, 2, 16, 128), bf),
+            pltpu.VMEM((32, 2, 16, 128), bf),
             pltpu.VMEM((NC, 8, 8, NX, 2, 16, 128), bf),
             pltpu.VMEM((NK, 512, 256), bf),
             pltpu.VMEM((1024, 256), bf),
@@ -381,10 +403,8 @@
             pltpu.VMEM((2, 512, 128), jnp.float32),
             dma((1,)),
             dma((2,)), dma((2,)),
-            dma((4,)), dma((4,)),
-            dma((8,)), dma((8,)),
-            dma((4,)), dma((4,)),
-            dma((8,)), dma((8,)),
+            dma((32,)), dma((32,)),
+            dma((32,)), dma((32,)),
             dma((2, 4, 2)), dma((2, 4, 2)),
             dma((8,)), dma((8,)),
             dma((2, 3)), dma((2, 3)),

time: 98 us -> 100 us (1.020); the launches traced: 96.4 us -> 99.8 us
  Pallas kernels: 92.6 us -> 96.1 us
    pallas_call x1, Pallas kernels: 92.6 us -> 96.1 us  [on_device(): pl.pallas_call(kernel, out_shape=jax.ShapeDtypeStruct((256, LB, 256), bf)...]
where the time goes in v4:
time: 100 us; the launch traced here: 99.8 us
  Pallas kernels  96.1 us (96%)
  local copies, waits for them, and re-layouts  3.05 us (3%)
    pallas_call x1, Pallas kernels, on_device(): pl.pallas_call(kernel, out_shape=jax.ShapeDtypeStruct((256, LB, 256), bf)...  96.1 us
    unnamed x1, local copies, waits for them, and re-layouts  3.05 us

profile of v4, /device:TPU:1, one launch (start us, length us, event | category | flops | bytes accessed | tf_op | source)
XLA Modules:
  0.0 99.8 jit_solution(7980728040717473034)
XLA Ops:
  0.7 96.1 %shard_map.28 = bf16[256,16,256]{2,1,0:T(8,128)(2,1)} custom-call(s32[1]{0:T(128)S(6)} %copy.4.owner_ref, bf16[2,8,32,256]{3,2,1,0:T(8,128)(2,1)} %spec_hbm.1), custom_call_target="tpu_custom_call" | custom-call | flops 17179869184 | bytes 3145728 | tf_op jit(solution)/shard_map/pallas_call | solution.py:383
  96.8 3.0 %copy.5 = bf16[256,16,256]{2,1,0:T(8,128)(2,1)} copy(bf16[256,16,256]{2,1,0:T(8,128)(2,1)} %shard_map.28) | data formatting | bytes 4194304
